TPU v7x, 128 devices: a whole 4x4x4 slice. The times are simulated.
128 devices in a mesh: fsdp: 16 (over x, y_hi, core), node: 8 (over y_lo, z).
Axes of the slice: x: 4, y: 4 (y_hi: 2, y_lo: 2; y = y_hi * 2 + y_lo), z: 4, core: 2. Of those that a mesh axis runs over, the one named last changes fastest.
Arguments:
- activations: bfloat16 [8192, 8192], P('fsdp', 'node'), may hold values from -6 to 6
- qkv_weight: bfloat16 [8192, 5120], P('fsdp', 'node'), may hold values from -0.09375 to 0.09375
- qkv_grad: bfloat16 [8192, 5120], P('fsdp', 'node'), may hold values from -6 to 6
Outputs:
- projected: bfloat16 [8192, 5120], P('fsdp', 'node')
- input_grad: bfloat16 [8192, 8192], P('fsdp', 'node')
- weight_grad: float32 [8192, 5120], P('fsdp', 'node')
All inputs are finite; a program needn't handle non-finite values.
Results may differ from a plain program's by a relative error of at most 0.017.
Values may be sent and summed in bfloat16 or wider, within the bound.
No kernel may reach another device: no remote copies, remote signals or barrier semaphores. Data moves between devices by JAX's collectives and lax.ppermute only.
A program may use at most 128 MiB of HBM per device.

v0:
```python
import jax
import jax.numpy as jnp
from jax import lax
from jax.sharding import PartitionSpec as P


def body(activations, qkv_weight, qkv_grad):
    gathered = lax.all_gather(activations, "node", axis=1, tiled=True)
    feature_cols = gathered
    forward = jnp.dot(
        feature_cols,
        lax.all_gather(qkv_weight, "fsdp", axis=0, tiled=True),
        preferred_element_type=jnp.float32,
    )
    partial_sum = lax.dot_general(
        qkv_grad,
        lax.all_gather(qkv_weight, "fsdp", axis=0, tiled=True),
        (((1,), (1,)), ((), ())),
        preferred_element_type=jnp.float32,
    )
    projected = forward.astype(jnp.bfloat16)
    input_grad = lax.psum_scatter(
        partial_sum.astype(jnp.bfloat16), "node", scatter_dimension=1, tiled=True
    )
    feature_cols = gathered
    weight_grad = lax.psum_scatter(
        lax.dot_general(
            feature_cols, qkv_grad, (((0,), (0,)), ((), ())), preferred_element_type=jnp.float32
        ).astype(jnp.bfloat16),
        "fsdp",
        scatter_dimension=0,
        tiled=True,
    ).astype(jnp.float32)
    return (projected, input_grad, weight_grad)


def solution(mesh):
    in_specs = (P("fsdp", "node"), P("fsdp", "node"), P("fsdp", "node"))
    out_specs = (P("fsdp", "node"), P("fsdp", "node"), P("fsdp", "node"))
    return jax.shard_map(body, mesh=mesh, in_specs=in_specs, out_specs=out_specs, check_vma=False)
```

profile of v0, /device:TPU:1, one launch (start us, length us, event | category | flops | bytes accessed | tf_op | source)
XLA Modules:
  0.0 403.2 jit_solution(3688470017451927738)
XLA Ops:
  7.2 0.0 copy-start
  7.2 0.0 all-gather.3.cloned.1.call-start
  7.2 0.7 all-gather.3.cloned.1.call-update
  7.9 0.0 all-gather.5.cloned.1.call-start
  8.0 0.7 all-gather.5.cloned.1.call-update
  8.7 0.0 reduce-scatter.5.cloned.1.call-start
  8.7 96.3 %all-gather.3.cloned.1.call-done = bf16[512,8192]{1,0:T(8,128)(2,1)} async-done(((bf16[512,1024]{1,0:T(8,128)(2,1)}), bf16[512,8192]{1,0:T(8,128)(2,1)}) %all-gather.3.cloned.1.call-update) | async-done | bytes 8388624 | tf_op jit(solution)/shard_map/all_gather | solution.py:8
  105.0 0.0 copy-done
  105.0 11.4 %convolution_convert_fusion = bf16[8192,640]{1,0:T(8,128)(2,1)} fusion(bf16[512,8192]{1,0:T(8,128)(2,1)} %all-gather.3.cloned.1.call-done, bf16[512,640]{1,0:T(8,128)(2,1)S(1)} %copy-done), kind=kOutput, calls=%fused_computation | convolution fusion | flops 5373952000 | bytes 19529728 | tf_op jit(solution)/shard_map/dot_general | solution.py:27
  116.4 0.0 reduce-scatter.5.cloned.1.call-update
  116.5 0.0 reduce-scatter.3.cloned.1.call-start
  116.5 71.4 %all-gather.5.cloned.1.call-done = bf16[8192,640]{1,0:T(8,128)(2,1)} async-done(((bf16[512,640]{1,0:T(8,128)(2,1)}), bf16[8192,640]{1,0:T(8,128)(2,1)}) %all-gather.5.cloned.1.call-update) | async-done | bytes 10485776 | tf_op jit(solution)/shard_map/all_gather | solution.py:12
  188.0 13.0 %convolution_convert_fusion.1 = bf16[512,8192]{1,0:T(8,128)(2,1)} fusion(bf16[512,640]{1,0:T(8,128)(2,1)S(1)} %copy-done, bf16[8192,640]{1,0:T(8,128)(2,1)} %all-gather.5.cloned.1.call-done), kind=kOutput, calls=%fused_computation.1 | convolution fusion | flops 5372903424 | bytes 19529728 | tf_op jit(solution)/shard_map/dot_general | solution.py:15
  200.9 0.0 reduce-scatter.3.cloned.1.call-update
  200.9 14.5 %convolution_convert_fusion.2 = bf16[512,640]{1,0:T(8,128)(2,1)} fusion(bf16[512,8192]{1,0:T(8,128)(2,1)} %all-gather.3.cloned.1.call-done, bf16[8192,640]{1,0:T(8,128)(2,1)} %all-gather.5.cloned.1.call-done), kind=kOutput, calls=%fused_computation.2 | convolution fusion | flops 5369036800 | bytes 19529728 | tf_op jit(solution)/shard_map/dot_general | solution.py:10
  215.5 85.6 %reduce-scatter.5.cloned.1.call-done = bf16[512,640]{1,0:T(8,128)(2,1)} async-done(((bf16[8192,640]{1,0:T(8,128)(2,1)}), bf16[512,640]{1,0:T(8,128)(2,1)}) %reduce-scatter.5.cloned.1.call-update) | async-done | bytes 655376 | tf_op jit(solution)/shard_map/reduce_scatter | solution.py:26
  301.1 2.2 convert_element_type.15
  303.3 93.3 %reduce-scatter.3.cloned.1.call-done = bf16[512,1024]{1,0:T(8,128)(2,1)} async-done(((bf16[512,8192]{1,0:T(8,128)(2,1)}), bf16[512,1024]{1,0:T(8,128)(2,1)}) %reduce-scatter.3.cloned.1.call-update) | async-done | bytes 1048592 | tf_op jit(solution)/shard_map/reduce_scatter | solution.py:22
Async XLA Ops:
  7.2 97.8 %copy-start = (bf16[512,640]{1,0:T(8,128)(2,1)S(1)}, bf16[512,640]{1,0:T(8,128)(2,1)}, u32[]{:S(2)}) copy-start(bf16[512,640]{1,0:T(8,128)(2,1)} %param.5) | copy-start | bytes 1966084
  7.2 97.8 %all-gather.3.cloned.1.call-start = ((), (), s32[]{:S(2)}) async-start(), calls=%async_computation.2 | async-start | bytes 9437184 | tf_op jit(solution)/shard_map/all_gather | solution.py:8
  7.9 180.0 %all-gather.5.cloned.1.call-start = ((), (), s32[]{:S(2)}) async-start(), calls=%async_computation.3 | async-start | bytes 11141120 | tf_op jit(solution)/shard_map/all_gather | solution.py:12
  8.7 292.4 %reduce-scatter.5.cloned.1.call-start = ((), (), s32[]{:S(2)}) async-start(), calls=%async_computation.5 | async-start | bytes 11141120 | tf_op jit(solution)/shard_map/reduce_scatter | solution.py:26
  116.5 280.2 %reduce-scatter.3.cloned.1.call-start = ((), (), s32[]{:S(2)}) async-start(), calls=%async_computation.4 | async-start | bytes 9437184 | tf_op jit(solution)/shard_map/reduce_scatter | solution.py:22
Sparse Core Ops, SparseCore 0:
  9.7 95.2 all-gather.2
  107.4 80.5 all-gather.4
  192.3 108.7 reduce-scatter.4
  304.1 92.5 reduce-scatter.2
where the time goes:
time: 403 us
  waiting for transfers between devices  348 us (86%)
  matrix products  38.9 us (10%)
  between operations  13.8 us (3%)
    all_gather x1, waiting for transfers between devices, body(): gathered = lax.all_gather(activations, 'node', axis=1, tiled=True)  96.3 us
    reduce_scatter x1, waiting for transfers between devices, body(): lax.psum_scatter(partial_sum.astype(jnp.bfloat16), 'node', scatter_dimens...  93.3 us
    reduce_scatter x1, waiting for transfers between devices, body(): lax.psum_scatter(lax.dot_general(feature_cols, qkv_grad, (((0,), (0,)), (...  85.6 us
    all_gather x1, waiting for transfers between devices, body(): lax.all_gather(qkv_weight, 'fsdp', axis=0, tiled=True)  71.4 us
    dot_general x1, matrix products, body(): jnp.dot(feature_cols, lax.all_gather(qkv_weight, 'fsdp', axis=0, tiled=Tr...  14.5 us
    dot_general x1, matrix products, body(): lax.dot_general(qkv_grad, lax.all_gather(qkv_weight, 'fsdp', axis=0, tile...  13 us
    dot_general x1, matrix products, body(): lax.dot_general(feature_cols, qkv_grad, (((0,), (0,)), ((), ())), preferr...  11.4 us
  transfers between devices with their start and end apart: 4, of which 4 were waited for; matrix products, arithmetic and copies ran while one was open for 10% of the time, Pallas kernels for 0%

commit v1 on v0

--- a/solution.py
+++ b/solution.py
@@ -5,7 +5,8 @@
 
 
 def body(activations, qkv_weight, qkv_grad):
-    gathered = lax.all_gather(activations, "node", axis=1, tiled=True)
+    sent = jnp.stack([activations] * lax.axis_size("node"))
+    gathered = jnp.concatenate(lax.all_to_all(sent, "node", 0, 0), axis=1)
     feature_cols = gathered
     forward = jnp.dot(
         feature_cols,

time: 403 us -> 372 us (0.923)
  waiting for transfers between devices: 348 us -> 179 us
  blocking collectives: 0 us -> 135 us
  local copies, waits for them, and re-layouts: 0.01 us -> 5.49 us
    all_to_all x0 -> x1, blocking collectives: none -> 135 us  [body(): gathered = jnp.concatenate(lax.all_to_all(sent, 'node', 0, 0), axis=1)]
    all_gather x1 -> x0, waiting for transfers between devices: 96.3 us -> none  [body(): gathered = lax.all_gather(activations, 'node', axis=1, tiled=True)]
    all_gather x1, waiting for transfers between devices: 71.4 us -> 0.02 us  [body(): lax.all_gather(qkv_weight, 'fsdp', axis=0, tiled=True)]
    unnamed x2 -> x5, local copies, waits for them, and re-layouts: 0.01 us -> 4.77 us
  transfers between devices with their start and end apart: 4 -> 3, of which waited for: 4 -> 2; matrix products, arithmetic and copies ran while one was open for 10% -> 11% of each run, Pallas kernels for 0% -> 0%
where the time goes in v1:
time: 372 us
  waiting for transfers between devices  179 us (48%)
  blocking collectives  135 us (36%)
  matrix products  36.7 us (10%)
  between operations  13.8 us (4%)
  local copies, waits for them, and re-layouts  5.49 us (1%)
    all_to_all x1, blocking collectives, body(): gathered = jnp.concatenate(lax.all_to_all(sent, 'node', 0, 0), axis=1)  135 us
    reduce_scatter x1, waiting for transfers between devices, body(): lax.psum_scatter(partial_sum.astype(jnp.bfloat16), 'node', scatter_dimens...  93.5 us
    reduce_scatter x1, waiting for transfers between devices, body(): lax.psum_scatter(lax.dot_general(feature_cols, qkv_grad, (((0,), (0,)), (...  84.5 us
    dot_general x1, matrix products, body(): jnp.dot(feature_cols, lax.all_gather(qkv_weight, 'fsdp', axis=0, tiled=Tr...  14.6 us
    dot_general x1, matrix products, body(): lax.dot_general(qkv_grad, lax.all_gather(qkv_weight, 'fsdp', axis=0, tile...  13 us
    dot_general x1, matrix products, body(): lax.dot_general(feature_cols, qkv_grad, (((0,), (0,)), ((), ())), preferr...  9.13 us
  transfers between devices with their start and end apart: 3, of which 2 were waited for; matrix products, arithmetic and copies ran while one was open for 11% of the time, Pallas kernels for 0%

profile of v1, /device:TPU:1, one launch (start us, length us, event | category | flops | bytes accessed | tf_op | source)
XLA Modules:
  0.0 371.9 jit_solution(7724117516742864224)
XLA Ops:
  7.2 0.0 copy-start
  7.2 0.0 all-gather.2.cloned.1.call-start
  7.2 0.7 all-gather.2.cloned.1.call-update
  7.9 0.0 reduce-scatter.5.cloned.1.call-start
  8.0 1.5 copy.6
  9.5 0.7 stack.2
  10.2 134.9 %all_to_all.5 = bf16[8,512,1024]{1,2,0:T(8,128)(2,1)S(1)} all-to-all(bf16[8,512,1024]{1,2,0:T(8,128)(2,1)S(1)} %stack.2), channel_id=1, replica_groups=mesh['fsdp'=16,'node'=8] {'node'}, dimensions={0} | all-to-all | bytes 16777216 | tf_op jit(solution)/shard_map/all_to_all | solution.py:9
  145.1 0.0 copy-start.1
  145.1 3.3 copy-done.1
  148.3 0.0 copy-done
  148.3 9.1 %convolution_convert_fusion = bf16[8192,640]{1,0:T(8,128)(2,1)} fusion(bf16[512,8192]{0,1:T(8,128)(2,1)S(1)} %bitcast.9, bf16[512,640]{1,0:T(8,128)(2,1)S(1)} %copy-done), kind=kOutput, calls=%fused_computation | convolution fusion | flops 5373952000 | bytes 19529728 | tf_op jit(solution)/shard_map/dot_general | solution.py:28
  157.5 0.0 reduce-scatter.5.cloned.1.call-update
  157.5 0.0 reduce-scatter.3.cloned.1.call-start
  157.5 0.0 all-gather.2.cloned.1.call-done
  157.6 13.0 %convolution_convert_fusion.1 = bf16[512,8192]{1,0:T(8,128)(2,1)} fusion(bf16[512,640]{1,0:T(8,128)(2,1)S(1)} %copy-done, bf16[8192,640]{1,0:T(8,128)(2,1)} %all-gather.2.cloned.1.call-done), kind=kOutput, calls=%fused_computation.1 | convolution fusion | flops 5372903424 | bytes 19529728 | tf_op jit(solution)/shard_map/dot_general | solution.py:16
  170.5 0.0 reduce-scatter.3.cloned.1.call-update
  170.6 14.6 %convolution_convert_fusion.2 = bf16[512,640]{1,0:T(8,128)(2,1)} fusion(bf16[512,8192]{0,1:T(8,128)(2,1)} %bitcast.10, bf16[8192,640]{1,0:T(8,128)(2,1)} %all-gather.2.cloned.1.call-done), kind=kOutput, calls=%fused_computation.2 | convolution fusion | flops 5369036800 | bytes 19529728 | tf_op jit(solution)/shard_map/dot_general | solution.py:11
  185.2 84.5 %reduce-scatter.5.cloned.1.call-done = bf16[512,640]{1,0:T(8,128)(2,1)} async-done(((bf16[8192,640]{1,0:T(8,128)(2,1)}), bf16[512,640]{1,0:T(8,128)(2,1)}) %reduce-scatter.5.cloned.1.call-update) | async-done | bytes 655376 | tf_op jit(solution)/shard_map/reduce_scatter | solution.py:27
  269.7 2.2 convert_element_type.15
  271.9 93.5 %reduce-scatter.3.cloned.1.call-done = bf16[512,1024]{1,0:T(8,128)(2,1)} async-done(((bf16[512,8192]{1,0:T(8,128)(2,1)}), bf16[512,1024]{1,0:T(8,128)(2,1)}) %reduce-scatter.3.cloned.1.call-update) | async-done | bytes 1048592 | tf_op jit(solution)/shard_map/reduce_scatter | solution.py:23
Async XLA Ops:
  7.2 141.2 %copy-start = (bf16[512,640]{1,0:T(8,128)(2,1)S(1)}, bf16[512,640]{1,0:T(8,128)(2,1)}, u32[]{:S(2)}) copy-start(bf16[512,640]{1,0:T(8,128)(2,1)} %param.5) | copy-start | bytes 1966084
  7.2 150.4 %all-gather.2.cloned.1.call-start = ((), (), s32[]{:S(2)}) async-start(), calls=%async_computation.3 | async-start | bytes 11141120 | tf_op jit(solution)/shard_map/all_gather | solution.py:13
  7.9 261.8 %reduce-scatter.5.cloned.1.call-start = ((), (), s32[]{:S(2)}) async-start(), calls=%async_computation.5 | async-start | bytes 11141120 | tf_op jit(solution)/shard_map/reduce_scatter | solution.py:27
  145.1 3.3 copy-start.1
  157.5 207.9 %reduce-scatter.3.cloned.1.call-start = ((), (), s32[]{:S(2)}) async-start(), calls=%async_computation.4 | async-start | bytes 9437184 | tf_op jit(solution)/shard_map/reduce_scatter | solution.py:23
Sparse Core Ops, SparseCore 0:
  10.4 120.6 all-gather.1
  157.6 112.0 reduce-scatter.4
  272.8 92.5 reduce-scatter.2
